TPU v7x, 32 devices: a whole 2x2x4 slice. The times are simulated.
32 devices in a mesh: leaf: 4 (over y, x), sub: 8 (over z, core).
Axes of the slice: x: 2, y: 2, z: 4, core: 2. Of those that a mesh axis runs over, the one named last changes fastest.
Arguments:
- points: float32 [1536, 3, 256], P(('leaf', 'sub')), may hold values from -1 to 1
- amplitude: float32 [1536, 256], P(('leaf', 'sub')), may hold values from 0.5 to 2
- vectors: float32 [1536, 8, 256], P(('leaf', 'sub')), may hold values from -6 to 6
- basis: float32 [1536, 256, 64], P(('leaf', 'sub')), may hold values from -0.375 to 0.375
- transfer: float32 [1536, 64, 64], P(('leaf', 'sub')), may hold values from -0.25 to 0.25
- couplings: float32 [1536, 16, 64, 64], P(('leaf', 'sub')), may hold values from -0.1875 to 0.1875
- coarse_couplings: float32 [192, 32, 64, 64], P(('leaf', 'sub')), may hold values from -0.125 to 0.125
- near_list: int32 [1536, 16], P(('leaf', 'sub')), may hold values from -1 to 1535, as said below
- far_list: int32 [1536, 16], P(('leaf', 'sub')), may hold values from -1 to 1535, as said below
- coarse_list: int32 [192, 32], P(('leaf', 'sub')), may hold values from -1 to 191, as said below
Outputs:
- product: float32 [1536, 8, 256], P(('leaf', 'sub'))
Inputs may be any that keep to these rules, and one draw needn't show every extreme that they name: `near_list`: slot 0 of leaf i is i itself; the other filled slots name distinct leaves within 48 positions of i in octree order; some leaves fill all 16 slots. `far_list`: filled slots name distinct leaves within 48 positions of i, none of them in leaf i's near list nor i itself; some leaves fill all 16 slots. `coarse_list`: filled slots name distinct parents other than p itself; filled slots come first, then -1; some parents fill all 32 slots.
All inputs are finite; a program needn't handle non-finite values.
Results may differ from a plain program's by a relative error of at most 0.0003.
Values sent between devices are 32-bit elements; how exact they have to be, the bound alone decides.
A program may use at most 128 MiB of HBM per device.

v0:
```python
import jax
import jax.numpy as jnp
from jax import lax
from jax.sharding import PartitionSpec as P

LEAF = 256
NEAR = 16


ELL2 = 0.25
HIGHEST_LEVEL = lax.Precision.HIGHEST
BLOCK_LEAVES = 4


def with_halo(cells, sides, width):
    for axis, dim in sides:
        count = lax.axis_size(axis)
        ends = count - 1
        head = lax.slice_in_dim(cells, 0, width, axis=dim)
        tail = lax.slice_in_dim(cells, cells.shape[dim] - width, cells.shape[dim], axis=dim)
        cells = jnp.concatenate(
            [
                lax.ppermute(tail, axis, [(i, (i + 1) % count) for i in range(ends)]),
                cells,
                lax.ppermute(head, axis, [((i + 1) % count, i) for i in range(ends)]),
            ],
            axis=dim,
        )
    return cells


def on_device(
    points,
    amplitude,
    vectors,
    basis,
    transfer,
    couplings,
    coarse_couplings,
    near_list,
    far_list,
    coarse_list,
):
    ldev = points.shape[0]
    leaf_size = points.shape[2]
    basis_rank = basis.shape[2]
    vector_count = vectors.shape[1]
    near_gain = 4.0 * (LEAF * NEAR) ** (-0.5)
    offset = lax.axis_index(("leaf", "sub")) * ldev - ldev
    stacked = jnp.concatenate([points, amplitude[:, None, :], vectors], axis=1)
    chans = stacked.shape[1]
    leaf_coefficients = jnp.einsum("lpr,lvp->lrv", basis, vectors, precision=HIGHEST_LEVEL)
    flat = leaf_coefficients.reshape(ldev, basis_rank * vector_count)
    neighbours = with_halo(stacked, ((("leaf", "sub"), 0),), ldev)
    coef_wide = with_halo(flat, ((("leaf", "sub"), 0),), ldev)

    def near_block(item):
        own, slots = item
        valid = slots >= 0
        local = jnp.where(valid, slots - offset, 0)
        other = neighbours[local]
        dist = jnp.zeros(other.shape[:2] + (leaf_size, leaf_size), jnp.float32)
        for comp in range(3):
            delta = own[:, None, comp, :, None] - other[:, :, comp, None, :]
            dist = dist + delta * delta
        kern = (
            jnp.exp(-dist / (2.0 * ELL2))
            * own[:, None, 3, :, None]
            * other[:, :, 3, None, :]
            * valid.astype(jnp.float32)[:, :, None, None]
        )
        return near_gain * jnp.einsum(
            "bnij,bnvj->bvi", kern, other[:, :, 4:], precision=HIGHEST_LEVEL
        )

    blocks = ldev // BLOCK_LEAVES
    near = lax.map(
        near_block,
        (
            stacked.reshape(blocks, BLOCK_LEAVES, chans, leaf_size),
            near_list.reshape(blocks, BLOCK_LEAVES, near_list.shape[1]),
        ),
    )
    near = near.reshape(ldev, vector_count, leaf_size)
    fvalid = far_list >= 0
    flocal = jnp.where(fvalid, far_list - offset, 0)
    got = (
        coef_wide[flocal].reshape(ldev, far_list.shape[1], basis_rank, vector_count)
        * fvalid.astype(jnp.float32)[:, :, None, None]
    )
    leaf_field = jnp.einsum("lkrs,lksv->lrv", couplings, got, precision=HIGHEST_LEVEL)
    parent_count = ldev // 8
    transposed_fourth = transfer.reshape(parent_count, 8, basis_rank, basis_rank)
    parent_coefficients = jnp.einsum(
        "xhjk,xhji->xki",
        transposed_fourth,
        leaf_coefficients.reshape(parent_count, 8, basis_rank, vector_count),
        precision=HIGHEST_LEVEL,
    )
    every_parent = lax.all_gather(
        parent_coefficients.reshape(parent_count, basis_rank * vector_count),
        ("leaf", "sub"),
        axis=0,
        tiled=True,
    )
    cvalid = coarse_list >= 0
    csafe = jnp.where(cvalid, coarse_list, 0)
    cgot = (
        every_parent[csafe].reshape(parent_count, coarse_list.shape[1], basis_rank, vector_count)
        * cvalid.astype(jnp.float32)[:, :, None, None]
    )
    parent_level_field = jnp.einsum(
        "pkst,pktv->psv", coarse_couplings, cgot, precision=HIGHEST_LEVEL
    )
    downward_pass = jnp.einsum(
        "oxzf,ofk->oxzk", transposed_fourth, parent_level_field, precision=HIGHEST_LEVEL
    ).reshape(ldev, basis_rank, vector_count)
    field = leaf_field + downward_pass
    far = jnp.einsum("lpr,lrv->lvp", basis, field, precision=HIGHEST_LEVEL)
    return near + far


def solution(mesh):
    placed = (
        P(("leaf", "sub"), None, None),
        P(("leaf", "sub"), None),
        P(("leaf", "sub"), None, None),
        P(("leaf", "sub"), None, None),
        P(("leaf", "sub"), None, None),
        P(("leaf", "sub"), None, None, None),
        P(("leaf", "sub"), None, None, None),
        P(("leaf", "sub"), None),
        P(("leaf", "sub"), None),
        P(("leaf", "sub"), None),
    )
    return jax.shard_map(
        on_device,
        mesh=mesh,
        in_specs=placed,
        out_specs=P(("leaf", "sub"), None, None),
        check_vma=False,
    )
```

profile of v0, /device:TPU:1, one launch (start us, length us, event | category | flops | bytes accessed | tf_op | source)
XLA Modules:
  0.0 506.3 jit_solution(2044178161846115916)
XLA Ops:
  1.9 4.4 fusion.42
  9.8 4.6 collective-permute-start.2
  19.0 3.6 collective-permute-start
  29.3 2.4 convolution_bitcast_fusion.1
  32.0 47.1 %all-gather = f32[32,6,512]{2,1,0:T(8,128)} all-gather(f32[1,6,512]{2,1,0:T(8,128)S(1)} %reshape.126), channel_id=1, replica_groups=mesh['leaf'=4,'sub'=8] {'leaf','sub'}, dimensions={0}, use_global_device_ids=true | all-gather | bytes 405504 | tf_op jit(solution)/shard_map/all_gather | solution.py:100
  85.1 2.7 reshape.92
  87.8 3.2 broadcast_multiply_fusion.1
  91.0 3.3 copy.42
  94.4 7.3 %fusion.43 = f32[6,8,64,1]{2,1,3,0:T(8,128)S(1)} fusion(f32[6,32,64,8]{2,3,1,0:T(8,128)} %copy.42, f32[6,32,64,64]{3,2,1,0:T(8,128)} %param.18), kind=kOutput, calls=%fused_computation.67 | convolution fusion | flops 75497472 | bytes 3551232 | tf_op jit(solution)/shard_map/pkst,pktv->psv/dot_general | solution.py:112
  101.7 4.4 fusion.44
  109.3 3.1 gather_fusion.1
  112.4 3.0 copy.37
  115.5 8.3 %reshape.88 = f32[48,16,64,8]{1,0,3,2:T(8,128)} reshape(f32[768,512]{0,1:T(8,128)} %copy.37) | data formatting | bytes 3145728 | tf_op jit(solution)/shard_map/reshape | solution.py:88
  123.7 10.8 %broadcast_multiply_fusion = f32[48,16,64,8]{1,0,3,2:T(8,128)} fusion(f32[48,16,64,8]{1,0,3,2:T(8,128)} %reshape.88, f32[48,16]{1,0:T(8,128)S(1)} %copy-done.12), kind=kLoop, calls=%fused_computation.47 | loop fusion | flops 393216 | bytes 3148800 | tf_op jit(solution)/shard_map/mul | solution.py:88
  134.5 10.7 %copy.39 = f32[48,16,64,8]{2,3,1,0:T(8,128)} copy(f32[48,16,64,8]{1,0,3,2:T(8,128)} %broadcast_multiply_fusion) | data formatting | bytes 3145728 | tf_op jit(solution)/shard_map/mul | solution.py:88
  145.2 23.5 %fusion.39 = f32[48,64,8]{1,2,0:T(8,128)S(1)} fusion(f32[48,64,8]{1,2,0:T(8,128)S(1)} %bitcast.107, f32[48,16,64,8]{2,3,1,0:T(8,128)} %copy.39, f32[48,16,64,64]{3,2,1,0:T(8,128)} %param.17), kind=kOutput, calls=%fused_computation.51 | convolution fusion | flops 302014464 | bytes 14352384 | tf_op jit(solution)/shard_map/lkrs,lksv->lrv/dot_general | solution.py:91
  170.1 2.5 copy.30
  172.6 330.4 %while.10 = (s32[]{:T(128)}, f32[12,4,8,256]{3,2,1,0:T(8,128)}, s32[12,4,16]{2,1,0:T(4,128)}, s32[]{:T(128)}, f32[144,12,256]{2,1,0:T(8,128)}, /*index=5*/f32[12,4,12,256]{3,1,2,0:T(4,128)}, s32[]{:T(128)}) while((s32[]{:T(128)}, f32[12,4,8,256]{3,2,1,0:T(8,128)}, s32[12,4,16]{2,1,0:T(4,128)}, s32[]{:T(128)}, f32[144,12,256]{2,1,0:T(8,128)}, ...), condition=%wide.region_1.2_spmd, body=%wide.region_0.1_spmd.sunk | while | flops 457188800 | bytes 3594969 | solution.py:77
  173.4 3.3 gather_fusion
  176.7 2.1 fusion.63
  179.6 20.6 %fusion.64 = f32[12,4,8,256]{3,2,1,0:T(8,128)} fusion(f32[12,4,8,256]{3,2,1,0:T(8,128)} %get-tuple-element.149, s32[]{:T(128)} %get-tuple-element.148, f32[4,16]{1,0:T(4,128)S(1)} %convert_bitcast_fusion.2, f32[4,16,256]{2,1,0:T(8,128)S(1)} %get-tuple-element.131, f32[4,256]{1,0:T(4,128)S(1)} %get-tuple-element.132, ...), kind=kOutput, calls=%fused_computation.31.clone.1 | convolution fusion | flops 457187328 | bytes 836352 | tf_op jit(solution)/shard_map/while/body/eval_jaxpr/bnij,bnvj->bvi/dot_general | solution.py:72
  200.9 3.3 gather_fusion
  204.2 2.1 fusion.63
  207.1 20.6 %fusion.64 = f32[12,4,8,256]{3,2,1,0:T(8,128)} fusion(f32[12,4,8,256]{3,2,1,0:T(8,128)} %get-tuple-element.149, s32[]{:T(128)} %get-tuple-element.148, f32[4,16]{1,0:T(4,128)S(1)} %convert_bitcast_fusion.2, f32[4,16,256]{2,1,0:T(8,128)S(1)} %get-tuple-element.131, f32[4,256]{1,0:T(4,128)S(1)} %get-tuple-element.132, ...), kind=kOutput, calls=%fused_computation.31.clone.1 | convolution fusion | flops 457187328 | bytes 836352 | tf_op jit(solution)/shard_map/while/body/eval_jaxpr/bnij,bnvj->bvi/dot_general | solution.py:72
  228.5 3.3 gather_fusion
  234.6 20.6 %fusion.64 = f32[12,4,8,256]{3,2,1,0:T(8,128)} fusion(f32[12,4,8,256]{3,2,1,0:T(8,128)} %get-tuple-element.149, s32[]{:T(128)} %get-tuple-element.148, f32[4,16]{1,0:T(4,128)S(1)} %convert_bitcast_fusion.2, f32[4,16,256]{2,1,0:T(8,128)S(1)} %get-tuple-element.131, f32[4,256]{1,0:T(4,128)S(1)} %get-tuple-element.132, ...), kind=kOutput, calls=%fused_computation.31.clone.1 | convolution fusion | flops 457187328 | bytes 836352 | tf_op jit(solution)/shard_map/while/body/eval_jaxpr/bnij,bnvj->bvi/dot_general | solution.py:72
  256.0 3.3 gather_fusion
  259.2 2.1 fusion.63
  262.2 20.6 %fusion.64 = f32[12,4,8,256]{3,2,1,0:T(8,128)} fusion(f32[12,4,8,256]{3,2,1,0:T(8,128)} %get-tuple-element.149, s32[]{:T(128)} %get-tuple-element.148, f32[4,16]{1,0:T(4,128)S(1)} %convert_bitcast_fusion.2, f32[4,16,256]{2,1,0:T(8,128)S(1)} %get-tuple-element.131, f32[4,256]{1,0:T(4,128)S(1)} %get-tuple-element.132, ...), kind=kOutput, calls=%fused_computation.31.clone.1 | convolution fusion | flops 457187328 | bytes 836352 | tf_op jit(solution)/shard_map/while/body/eval_jaxpr/bnij,bnvj->bvi/dot_general | solution.py:72
  283.5 3.3 gather_fusion
  289.7 20.6 %fusion.64 = f32[12,4,8,256]{3,2,1,0:T(8,128)} fusion(f32[12,4,8,256]{3,2,1,0:T(8,128)} %get-tuple-element.149, s32[]{:T(128)} %get-tuple-element.148, f32[4,16]{1,0:T(4,128)S(1)} %convert_bitcast_fusion.2, f32[4,16,256]{2,1,0:T(8,128)S(1)} %get-tuple-element.131, f32[4,256]{1,0:T(4,128)S(1)} %get-tuple-element.132, ...), kind=kOutput, calls=%fused_computation.31.clone.1 | convolution fusion | flops 457187328 | bytes 836352 | tf_op jit(solution)/shard_map/while/body/eval_jaxpr/bnij,bnvj->bvi/dot_general | solution.py:72
  311.0 3.3 gather_fusion
  314.3 2.1 fusion.63
  317.2 20.6 %fusion.64 = f32[12,4,8,256]{3,2,1,0:T(8,128)} fusion(f32[12,4,8,256]{3,2,1,0:T(8,128)} %get-tuple-element.149, s32[]{:T(128)} %get-tuple-element.148, f32[4,16]{1,0:T(4,128)S(1)} %convert_bitcast_fusion.2, f32[4,16,256]{2,1,0:T(8,128)S(1)} %get-tuple-element.131, f32[4,256]{1,0:T(4,128)S(1)} %get-tuple-element.132, ...), kind=kOutput, calls=%fused_computation.31.clone.1 | convolution fusion | flops 457187328 | bytes 836352 | tf_op jit(solution)/shard_map/while/body/eval_jaxpr/bnij,bnvj->bvi/dot_general | solution.py:72
  338.6 3.3 gather_fusion
  344.8 20.6 %fusion.64 = f32[12,4,8,256]{3,2,1,0:T(8,128)} fusion(f32[12,4,8,256]{3,2,1,0:T(8,128)} %get-tuple-element.149, s32[]{:T(128)} %get-tuple-element.148, f32[4,16]{1,0:T(4,128)S(1)} %convert_bitcast_fusion.2, f32[4,16,256]{2,1,0:T(8,128)S(1)} %get-tuple-element.131, f32[4,256]{1,0:T(4,128)S(1)} %get-tuple-element.132, ...), kind=kOutput, calls=%fused_computation.31.clone.1 | convolution fusion | flops 457187328 | bytes 836352 | tf_op jit(solution)/shard_map/while/body/eval_jaxpr/bnij,bnvj->bvi/dot_general | solution.py:72
  366.1 3.3 gather_fusion
  372.3 20.6 %fusion.64 = f32[12,4,8,256]{3,2,1,0:T(8,128)} fusion(f32[12,4,8,256]{3,2,1,0:T(8,128)} %get-tuple-element.149, s32[]{:T(128)} %get-tuple-element.148, f32[4,16]{1,0:T(4,128)S(1)} %convert_bitcast_fusion.2, f32[4,16,256]{2,1,0:T(8,128)S(1)} %get-tuple-element.131, f32[4,256]{1,0:T(4,128)S(1)} %get-tuple-element.132, ...), kind=kOutput, calls=%fused_computation.31.clone.1 | convolution fusion | flops 457187328 | bytes 836352 | tf_op jit(solution)/shard_map/while/body/eval_jaxpr/bnij,bnvj->bvi/dot_general | solution.py:72
  393.6 3.3 gather_fusion
  396.9 2.1 fusion.63
  399.8 20.6 %fusion.64 = f32[12,4,8,256]{3,2,1,0:T(8,128)} fusion(f32[12,4,8,256]{3,2,1,0:T(8,128)} %get-tuple-element.149, s32[]{:T(128)} %get-tuple-element.148, f32[4,16]{1,0:T(4,128)S(1)} %convert_bitcast_fusion.2, f32[4,16,256]{2,1,0:T(8,128)S(1)} %get-tuple-element.131, f32[4,256]{1,0:T(4,128)S(1)} %get-tuple-element.132, ...), kind=kOutput, calls=%fused_computation.31.clone.1 | convolution fusion | flops 457187328 | bytes 836352 | tf_op jit(solution)/shard_map/while/body/eval_jaxpr/bnij,bnvj->bvi/dot_general | solution.py:72
  421.2 3.3 gather_fusion
  427.4 20.6 %fusion.64 = f32[12,4,8,256]{3,2,1,0:T(8,128)} fusion(f32[12,4,8,256]{3,2,1,0:T(8,128)} %get-tuple-element.149, s32[]{:T(128)} %get-tuple-element.148, f32[4,16]{1,0:T(4,128)S(1)} %convert_bitcast_fusion.2, f32[4,16,256]{2,1,0:T(8,128)S(1)} %get-tuple-element.131, f32[4,256]{1,0:T(4,128)S(1)} %get-tuple-element.132, ...), kind=kOutput, calls=%fused_computation.31.clone.1 | convolution fusion | flops 457187328 | bytes 836352 | tf_op jit(solution)/shard_map/while/body/eval_jaxpr/bnij,bnvj->bvi/dot_general | solution.py:72
  448.7 3.3 gather_fusion
  454.9 20.6 %fusion.64 = f32[12,4,8,256]{3,2,1,0:T(8,128)} fusion(f32[12,4,8,256]{3,2,1,0:T(8,128)} %get-tuple-element.149, s32[]{:T(128)} %get-tuple-element.148, f32[4,16]{1,0:T(4,128)S(1)} %convert_bitcast_fusion.2, f32[4,16,256]{2,1,0:T(8,128)S(1)} %get-tuple-element.131, f32[4,256]{1,0:T(4,128)S(1)} %get-tuple-element.132, ...), kind=kOutput, calls=%fused_computation.31.clone.1 | convolution fusion | flops 457187328 | bytes 836352 | tf_op jit(solution)/shard_map/while/body/eval_jaxpr/bnij,bnvj->bvi/dot_general | solution.py:72
  476.2 3.3 gather_fusion
  482.4 20.6 %fusion.64 = f32[12,4,8,256]{3,2,1,0:T(8,128)} fusion(f32[12,4,8,256]{3,2,1,0:T(8,128)} %get-tuple-element.149, s32[]{:T(128)} %get-tuple-element.148, f32[4,16]{1,0:T(4,128)S(1)} %convert_bitcast_fusion.2, f32[4,16,256]{2,1,0:T(8,128)S(1)} %get-tuple-element.131, f32[4,256]{1,0:T(4,128)S(1)} %get-tuple-element.132, ...), kind=kOutput, calls=%fused_computation.31.clone.1 | convolution fusion | flops 457187328 | bytes 836352 | tf_op jit(solution)/shard_map/while/body/eval_jaxpr/bnij,bnvj->bvi/dot_general | solution.py:72
  503.0 3.4 convolution_add_fusion
  (168 shorter events, 61.0 us)
Async XLA Ops:
  0.0 1.9 copy-start
  0.0 16.3 %copy-start.2 = (f32[48,8,256]{2,1,0:T(8,128)S(1)}, f32[48,8,256]{2,1,0:T(8,128)}, u32[]{:S(2)}) copy-start(f32[48,8,256]{2,1,0:T(8,128)} %param.14) | copy-start | bytes 1179652
  0.0 24.6 %copy-start.14 = (s32[6,32]{1,0:T(8,128)S(1)}, s32[6,32]{1,0:T(8,128)}, u32[]{:S(2)}) copy-start(s32[6,32]{1,0:T(8,128)} %param.21) | copy-start | bytes 2308
  0.0 28.4 %copy-start.13 = (s32[48,16]{0,1:T(8,128)S(1)}, s32[48,16]{0,1:T(8,128)}, u32[]{:S(2)}) copy-start(s32[48,16]{0,1:T(8,128)} %param.20) | copy-start | bytes 9220
  9.8 98.5 %collective-permute-start.2 = (f32[48,512]{1,0:T(8,128)}, f32[48,512]{1,0:T(8,128)}, u32[]{:S(2)}, u32[]{:S(2)}) collective-permute-start(f32[48,512]{1,0:T(8,128)} %copy.33), channel_id=1, source_target_pairs={{0,1},{1,2},{2,3},{3,4},{4,5},{5,6},{6,7},{7,8},{8,9},{9,10},{10,1... | collective-permute-start | bytes 294920 | tf_op jit(solution)/shard_map/ppermute | solution.py:23
  14.4 93.9 %collective-permute-start.3 = (f32[48,512]{1,0:T(8,128)}, f32[48,512]{1,0:T(8,128)}, u32[]{:S(2)}, u32[]{:S(2)}) collective-permute-start(f32[48,512]{1,0:T(8,128)} %copy.33), channel_id=1, source_target_pairs={{1,0},{2,1},{3,2},{4,3},{5,4},{6,5},{7,6},{8,7},{9,8},{10,9},{11,1... | collective-permute-start | bytes 294920 | tf_op jit(solution)/shard_map/ppermute | solution.py:25
  16.5 0.8 copy-start.4
  19.0 149.7 %collective-permute-start = (f32[48,12,256]{2,0,1:T(8,128)}, f32[48,12,256]{2,0,1:T(8,128)}, u32[]{:S(2)}, u32[]{:S(2)}) collective-permute-start(f32[48,12,256]{2,0,1:T(8,128)} %pad_maximum_fusion.2), channel_id=1, source_target_pairs={{0,1},{1,2},{2,3},{3,4},{4,5},{5,6},{6,7},{7,8},{8,9},{9,10},{10,1... | collective-permute-start | bytes 1769480 | tf_op jit(solution)/shard_map/ppermute | solution.py:23
  22.6 146.1 %collective-permute-start.1 = (f32[48,12,256]{2,0,1:T(8,128)}, f32[48,12,256]{2,0,1:T(8,128)}, u32[]{:S(2)}, u32[]{:S(2)}) collective-permute-start(f32[48,12,256]{2,0,1:T(8,128)} %pad_maximum_fusion.2), channel_id=1, source_target_pairs={{1,0},{2,1},{3,2},{4,3},{5,4},{6,5},{7,6},{8,7},{9,8},{10,9},{11,1... | collective-permute-start | bytes 1769480 | tf_op jit(solution)/shard_map/ppermute | solution.py:25
  94.4 7.3 %copy-start.1 = (f32[48,64,64]{2,1,0:T(8,128)S(1)}, f32[48,64,64]{2,1,0:T(8,128)}, u32[]{:S(2)}) copy-start(f32[48,64,64]{2,1,0:T(8,128)} %param.16) | copy-start | bytes 2359300
  94.4 11.8 %copy-start.3 = (f32[48,8,256]{2,1,0:T(8,128)S(1)}, f32[48,8,256]{2,1,0:T(8,128)}, u32[]{:S(2)}) copy-start(f32[48,8,256]{2,1,0:T(8,128)} %param.14) | copy-start | bytes 1179652
  94.4 11.8 %copy-start.8 = (f32[48,3,256]{2,1,0:T(4,128)S(1)}, f32[48,3,256]{2,1,0:T(4,128)}, u32[]{:S(2)}) copy-start(f32[48,3,256]{2,1,0:T(4,128)} %copy.48) | copy-start | bytes 442372
  94.4 11.8 %copy-start.11 = (f32[12,4,1,256]{3,2,1,0:T(1,128)S(1)}, f32[12,4,1,256]{3,2,1,0:T(1,128)}, u32[]{:S(2)}) copy-start(f32[12,4,1,256]{3,2,1,0:T(1,128)} %concatenate.21) | copy-start | bytes 147460
  101.7 5.9 %copy-start.15 = (s32[48,16]{0,1:T(8,128)S(1)}, s32[48,16]{0,1:T(8,128)}, u32[]{:S(2)}) copy-start(s32[48,16]{0,1:T(8,128)} %param.19) | copy-start | bytes 9220
  101.7 6.6 %copy-start.10 = (f32[48,512]{1,0:T(8,128)S(1)}, f32[48,512]{1,0:T(8,128)}, u32[]{:S(2)}) copy-start(f32[48,512]{1,0:T(8,128)} %copy.33) | copy-start | bytes 294916
  115.5 8.3 %copy-start.12 = (f32[48,16]{1,0:T(8,128)S(1)}, f32[48,16]{1,0:T(8,128)}, u32[]{:S(2)}) copy-start(f32[48,16]{1,0:T(8,128)} %copy.38) | copy-start | bytes 9220
  134.5 10.7 %copy-start.7 = (f32[6,8,8,64]{3,1,2,0:T(8,128)S(1)}, f32[6,8,8,64]{3,1,2,0:T(8,128)}, u32[]{:S(2)}) copy-start(f32[6,8,8,64]{3,1,2,0:T(8,128)} %fusion.44) | copy-start | bytes 294916
  145.2 23.5 %copy-start.5 = (f32[48,8,256]{2,0,1:T(8,128)S(1)}, f32[48,8,256]{2,0,1:T(8,128)}, u32[]{:S(2)}) copy-start(f32[48,8,256]{2,0,1:T(8,128)} %copy-done.4) | copy-start | bytes 1179652
  145.2 23.5 %copy-start.6 = (f32[48,3,256]{2,0,1:T(8,128)S(1)}, f32[48,3,256]{2,0,1:T(8,128)}, u32[]{:S(2)}) copy-start(f32[48,3,256]{2,0,1:T(8,128)} %param.12) | copy-start | bytes 442372
  145.2 23.5 %copy-start.9 = (f32[48,256]{1,0:T(8,128)S(1)}, f32[48,256]{1,0:T(8,128)}, u32[]{:S(2)}) copy-start(f32[48,256]{1,0:T(8,128)} %param.13) | copy-start | bytes 147460
where the time goes:
time: 511 us; the launch traced here: 506 us
  matrix products  292 us (57%)
  local copies, waits for them, and re-layouts  126 us (25%)
  blocking collectives  47.1 us (9%)
  other arithmetic  28 us (5%)
  starting transfers between devices  12.1 us (2%)
    dot_general x12, matrix products, near_block(): jnp.einsum('bnij,bnvj->bvi', kern, other[:, :, 4:], precision=HIGHEST_LEVEL)  247 us
    all_gather x1, blocking collectives, on_device(): lax.all_gather(parent_coefficients.reshape(parent_count, basis_rank * vec...  47.1 us
    gather x12, local copies, waits for them, and re-layouts, near_block(): other = neighbours[local]  39.2 us
    slice x12, local copies, waits for them, and re-layouts, near_block(): delta = own[:, None, comp, :, None] - other[:, :, comp, None, :]  24.6 us
    dot_general x1, matrix products, on_device(): jnp.einsum('lkrs,lksv->lrv', couplings, got, precision=HIGHEST_LEVEL)  23.5 us
    mul x1, other arithmetic, on_device(): coef_wide[flocal].reshape(ldev, far_list.shape[1], basis_rank, vector_count)  10.8 us
    mul x1, local copies, waits for them, and re-layouts, on_device(): coef_wide[flocal].reshape(ldev, far_list.shape[1], basis_rank, vector_count)  10.7 us
  transfers between devices with their start and end apart: 4, of which 0 were waited for; matrix products, arithmetic and copies ran while one was open for 19% of the time, Pallas kernels for 0%

commit v1 on v0

v1 whole, which is shorter than its diff:
```python
import math

import jax
import jax.numpy as jnp
from jax import lax
from jax.experimental import pallas as pl
from jax.experimental.pallas import tpu as pltpu
from jax.sharding import PartitionSpec as P

LEAF = 256
NEAR = 16
ELL2 = 0.25
AXES = ("leaf", "sub")
CHILDREN = 8
FEATURES = 32
VMEM_BYTES = 56 * 1024 * 1024
f32 = jnp.float32
bf16 = jnp.bfloat16


def halo(cells):
    ends = lax.axis_size(AXES) - 1
    before = lax.ppermute(cells, AXES, [(i, i + 1) for i in range(ends)])
    after = lax.ppermute(cells, AXES, [(i + 1, i) for i in range(ends)])
    return before, after


def three(x):
    high = x.astype(bf16).astype(f32)
    rest = x - high
    mid = rest.astype(bf16).astype(f32)
    return high, mid, rest - mid


def split(x):
    high = x.astype(bf16)
    return high, (x - high.astype(f32)).astype(bf16)


def stacked_rows(x):
    high = x.astype(bf16).astype(f32)
    return jnp.concatenate([high, x - high], axis=0).astype(bf16)


def dot(a, b):
    return jnp.dot(a, b, preferred_element_type=f32)


def dot_t(a, b):
    return lax.dot_general(a, b, (((1,), (1,)), ((), ())), preferred_element_type=f32)


def folded(x):
    half = x.shape[0] // 2
    return x[:half] + x[half:]


def up_kernel(vectors, basis, transfer, coefs, parents):
    total = jnp.zeros((16, transfer.shape[2]), f32)
    for q in range(CHILDREN):
        high, low = split(basis[q])
        rows = stacked_rows(vectors[q])
        one = folded(dot_t(rows, high) + dot_t(rows, low))
        coefs[q] = one
        rows = stacked_rows(one)
        high, low = split(transfer[q])
        total = total + dot(rows, high) + dot(rows, low)
    parents[0] = folded(total)


def pieces(points, at):
    scale = math.sqrt(math.log2(math.e) / ELL2)
    rows = [points[c, pl.ds(at, 1), :] for c in range(3)]
    x = jnp.concatenate(rows, axis=0) * scale
    norm = -0.5 * jnp.sum(x * x, axis=0, keepdims=True)
    ones = jnp.ones((3, x.shape[1]), f32)
    rest = jnp.zeros((FEATURES - 24, x.shape[1]), f32)
    return three(x), three(norm), ones, rest


def own_features(points, at):
    (h, m, l), norm, ones, rest = pieces(points, at)
    return jnp.concatenate([h, m, h, l, h, m, *norm, ones, rest], axis=0).astype(bf16)


def other_features(points, at):
    (h, m, l), norm, ones, rest = pieces(points, at)
    rows = jnp.concatenate([h, h, m, h, l, m, ones, *norm, rest], axis=0)
    return jnp.transpose(rows).astype(bf16)


def near_kernel(
    slots,
    points_before,
    points_own,
    points_after,
    vectors_before,
    vectors_own,
    vectors_after,
    out,
    others,
    values,
    filled,
):
    blank = others.shape[0] - 1
    base = pl.program_id(0) * CHILDREN
    ldev = blank // 3

    @pl.when(pl.program_id(0) == 0)
    def _():
        sides = (
            (points_before, vectors_before),
            (points_own, vectors_own),
            (points_after, vectors_after),
        )

        def prepare(at, carry):
            for side, (points, vectors) in enumerate(sides):
                where = side * ldev + at
                others[where] = other_features(points, at)
                values[where] = stacked_rows(vectors[at] * points[3, pl.ds(at, 1), :])
            return carry

        lax.fori_loop(0, ldev, prepare, 0)
        others[blank] = jnp.zeros(others.shape[1:], bf16)
        values[blank] = jnp.zeros(values.shape[1:], bf16)

    gain = 4.0 * (LEAF * NEAR) ** (-0.5)
    width = slots.shape[1]

    def leaf(q, carry):
        count = jnp.int32(0)
        for n in range(width):
            j = slots[base + q, n]
            filled[count] = j
            count = count + jnp.where(j < blank, 1, 0)
        for n in range(3):
            filled[count + n] = blank
        mine = own_features(points_own, base + q)

        def some(first, many, total):
            for u in range(many):
                j = filled[first + u]
                kern = jnp.exp2(dot(others[j], mine))
                high, low = split(kern)
                rows = values[j]
                total = total + dot(rows, high) + dot(rows, low)
            return total

        total = jnp.zeros((16, out.shape[2]), f32)
        fours = (count + 1) // 4
        total = lax.fori_loop(0, fours, lambda g, t: some(4 * g, 4, t), total)
        twos = jnp.where(count > 4 * fours, 1, 0)
        total = lax.fori_loop(0, twos, lambda g, t: some(4 * fours, 2, t), total)
        out[q] = folded(total) * (gain * points_own[3, pl.ds(base + q, 1), :])
        return carry

    lax.fori_loop(0, CHILDREN, leaf, 0)


def coupled(index, slots, table, matrix):
    rank = table.shape[2]
    total = jnp.zeros((64, 4 * rank), f32)
    for g in range(slots.shape[1] // 4):
        rows = jnp.concatenate([table[slots[index, 4 * g + u]] for u in range(4)], axis=0)
        high, low = split(matrix(4 * g))
        total = total + dot_t(rows, high) + dot_t(rows, low)
    blocks = [total[16 * u : 16 * u + 16, rank * u : rank * u + rank] for u in range(4)]
    return folded(blocks[0] + blocks[1] + blocks[2] + blocks[3])


def far_kernel(
    far_slots,
    coarse_slots,
    coefs_before,
    coefs_own,
    coefs_after,
    every,
    couplings,
    coarse,
    transfer,
    basis,
    near,
    out,
    coefs,
    parents,
):
    rank = transfer.shape[2]
    step = pl.program_id(0)
    ldev = coefs_own.shape[0]

    @pl.when(step == 0)
    def _():
        def prepare(at, carry):
            coefs[at] = stacked_rows(coefs_before[at])
            coefs[ldev + at] = stacked_rows(coefs_own[at])
            coefs[2 * ldev + at] = stacked_rows(coefs_after[at])
            return carry

        def prepare_parent(at, carry):
            parents[at] = stacked_rows(every[at])
            return carry

        lax.fori_loop(0, ldev, prepare, 0, unroll=2)
        lax.fori_loop(0, every.shape[0], prepare_parent, 0, unroll=4)
        coefs[3 * ldev] = jnp.zeros(coefs.shape[1:], bf16)
        parents[every.shape[0]] = jnp.zeros(parents.shape[1:], bf16)

    field = coupled(
        step, coarse_slots, parents, lambda k: coarse[0, k : k + 4].reshape(4 * rank, rank)
    )
    above = stacked_rows(field)

    def leaf(q, carry):
        field = coupled(
            step * CHILDREN + q,
            far_slots,
            coefs,
            lambda k: couplings[q, k : k + 4].reshape(4 * rank, rank),
        )
        high, low = split(transfer[q])
        field = field + folded(dot_t(above, high) + dot_t(above, low))
        rows = stacked_rows(field)
        high, low = split(basis[q])
        out[q] = near[q] + folded(dot(rows, high) + dot(rows, low))
        return carry

    lax.fori_loop(0, CHILDREN, leaf, 0)


def whole(x):
    return pl.BlockSpec(x.shape, lambda i: (0,) * x.ndim)


def part(x, rows):
    return pl.BlockSpec((rows,) + x.shape[1:], lambda i: (i,) + (0,) * (x.ndim - 1))


def scalars():
    return pl.BlockSpec(memory_space=pltpu.SMEM)


def params():
    return pltpu.CompilerParams(vmem_limit_bytes=VMEM_BYTES)


def on_device(
    points,
    amplitude,
    vectors,
    basis,
    transfer,
    couplings,
    coarse_couplings,
    near_list,
    far_list,
    coarse_list,
):
    ldev, _, leaf_size = points.shape
    rank = transfer.shape[2]
    count = vectors.shape[1]
    nparents = ldev // CHILDREN
    offset = lax.axis_index(AXES) * ldev - ldev
    blank = 3 * ldev

    basis = basis.swapaxes(1, 2)
    sites = jnp.concatenate([points.swapaxes(0, 1), amplitude[None]], axis=0)
    points_before, points_after = halo(sites)
    vectors_before, vectors_after = halo(vectors)

    coefs, parents = pl.pallas_call(
        up_kernel,
        grid=(nparents,),
        out_shape=(
            jax.ShapeDtypeStruct((ldev, count, rank), f32),
            jax.ShapeDtypeStruct((nparents, count, rank), f32),
        ),
        in_specs=[part(vectors, CHILDREN), part(basis, CHILDREN), part(transfer, CHILDREN)],
        out_specs=(
            pl.BlockSpec((CHILDREN, count, rank), lambda i: (i, 0, 0)),
            pl.BlockSpec((1, count, rank), lambda i: (i, 0, 0)),
        ),
        compiler_params=params(),
        cost_estimate=pl.CostEstimate(
            flops=8 * ldev * leaf_size * rank * 16,
            bytes_accessed=12 * ldev * leaf_size * rank,
            transcendentals=0,
        ),
        name="upward",
    )(vectors, basis, transfer)

    every = lax.all_gather(parents, AXES, axis=0, tiled=True)
    coefs_before, coefs_after = halo(coefs)

    near_slots = jnp.where(near_list >= 0, near_list - offset, blank)
    far_slots = jnp.where(far_list >= 0, far_list - offset, blank)
    coarse_slots = jnp.where(coarse_list >= 0, coarse_list, every.shape[0])

    pairs = ldev * near_list.shape[1]
    near = pl.pallas_call(
        near_kernel,
        grid=(nparents,),
        out_shape=jax.ShapeDtypeStruct((ldev, count, leaf_size), f32),
        in_specs=[scalars()] + [whole(sites)] * 3 + [whole(vectors)] * 3,
        out_specs=pl.BlockSpec((CHILDREN, count, leaf_size), lambda i: (i, 0, 0)),
        scratch_shapes=[
            pltpu.VMEM((blank + 1, leaf_size, FEATURES), bf16),
            pltpu.VMEM((blank + 1, 2 * count, leaf_size), bf16),
            pltpu.SMEM((near_list.shape[1] + 8,), jnp.int32),
        ],
        compiler_params=params(),
        cost_estimate=pl.CostEstimate(
            flops=pairs * leaf_size * leaf_size * 512,
            bytes_accessed=20 * vectors.size,
            transcendentals=pairs * leaf_size * leaf_size,
        ),
        name="near_field",
    )(
        near_slots,
        points_before,
        sites,
        points_after,
        vectors_before,
        vectors,
        vectors_after,
    )

    return pl.pallas_call(
        far_kernel,
        grid=(nparents,),
        out_shape=jax.ShapeDtypeStruct((ldev, count, leaf_size), f32),
        in_specs=[
            scalars(),
            scalars(),
            whole(coefs),
            whole(coefs),
            whole(coefs),
            whole(every),
            part(couplings, CHILDREN),
            part(coarse_couplings, 1),
            part(transfer, CHILDREN),
            part(basis, CHILDREN),
            part(near, CHILDREN),
        ],
        out_specs=pl.BlockSpec((CHILDREN, count, leaf_size), lambda i: (i, 0, 0)),
        scratch_shapes=[
            pltpu.VMEM((blank + 1, 2 * count, rank), bf16),
            pltpu.VMEM((every.shape[0] + 1, 2 * count, rank), bf16),
        ],
        compiler_params=params(),
        cost_estimate=pl.CostEstimate(
            flops=couplings.size * 64,
            bytes_accessed=8 * couplings.size,
            transcendentals=0,
        ),
        name="far_field",
    )(
        far_slots,
        coarse_slots,
        coefs_before,
        coefs,
        coefs_after,
        every,
        couplings,
        coarse_couplings,
        transfer,
        basis,
        near,
    )


def solution(mesh):
    three_d = P(AXES, None, None)
    placed = (
        three_d,
        P(AXES, None),
        three_d,
        three_d,
        three_d,
        P(AXES, None, None, None),
        P(AXES, None, None, None),
        P(AXES, None),
        P(AXES, None),
        P(AXES, None),
    )
    return jax.shard_map(
        on_device,
        mesh=mesh,
        in_specs=placed,
        out_specs=three_d,
        check_vma=False,
    )
```

time: 511 us -> 217 us (0.42)
  matrix products: 292 us -> 0 us
  Pallas kernels: 0 us -> 143 us
  local copies, waits for them, and re-layouts: 126 us -> 3.2 us
  other arithmetic: 28 us -> 2.85 us
  starting transfers between devices: 12.1 us -> 17.8 us
    dot_general x18 -> x0, matrix products: 292 us -> none  [the longest x12 247 us: near_block(): jnp.einsum('bnij,bnvj->bvi', kern, other[:, :, 4:], precision=HIGHEST_LEVEL)]
    pallas_call x0 -> x3, Pallas kernels: none -> 143 us  [the longest x1 102 us: on_device(): pl.pallas_call(near_kernel, grid=(nparents,), out_shape=jax.ShapeDtypeStr...]
    gather x16 -> x0, local copies, waits for them, and re-layouts: 49 us -> none  [the longest x12 39.2 us: near_block(): other = neighbours[local]]
    slice x12 -> x0, local copies, waits for them, and re-layouts: 24.6 us -> none  [near_block(): delta = own[:, None, comp, :, None] - other[:, :, comp, None, :]]
    mul x2 -> x0, other arithmetic: 14 us -> none  [the longest x1 10.8 us: on_device(): coef_wide[flocal].reshape(ldev, far_list.shape[1], basis_rank, vector_count)]
    mul x2 -> x0, local copies, waits for them, and re-layouts: 14 us -> none  [the longest x1 10.7 us: on_device(): coef_wide[flocal].reshape(ldev, far_list.shape[1], basis_rank, vector_count)]
    reshape x3 -> x0, local copies, waits for them, and re-layouts: 12.6 us -> none  [the longest x1 8.26 us: on_device(): coef_wide[flocal].reshape(ldev, far_list.shape[1], basis_rank, vector_count)]
    squeeze x12 -> x0, local copies, waits for them, and re-layouts: 9.71 us -> none  [on_device(): lax.map(near_block, (stacked.reshape(blocks, BLOCK_LEAVES, chans, leaf_si...]
  transfers between devices with their start and end apart: 4 -> 6, of which waited for: 0 -> 0; matrix products, arithmetic and copies ran while one was open for 19% -> 2% of each run, Pallas kernels for 0% -> 51%
where the time goes in v1:
time: 217 us; the launch traced here: 214 us
  Pallas kernels  143 us (66%)
  blocking collectives  46.6 us (21%)
  starting transfers between devices  17.8 us (8%)
  local copies, waits for them, and re-layouts  3.2 us (1%)
  other arithmetic  2.85 us (1%)
    pallas_call x1, Pallas kernels, on_device(): pl.pallas_call(near_kernel, grid=(nparents,), out_shape=jax.ShapeDtypeStr...  102 us
    all_gather x1, blocking collectives, on_device(): every = lax.all_gather(parents, AXES, axis=0, tiled=True)  46.6 us
    pallas_call x1, Pallas kernels, on_device(): pl.pallas_call(far_kernel, grid=(nparents,), out_shape=jax.ShapeDtypeStru...  34.2 us
    ppermute x3, starting transfers between devices, halo(): before = lax.ppermute(cells, AXES, [(i, i + 1) for i in range(ends)])  11.9 us
    pallas_call x1, Pallas kernels, on_device(): pl.pallas_call(up_kernel, grid=(nparents,), out_shape=(jax.ShapeDtypeStru...  6.92 us
    ppermute x3, starting transfers between devices, halo(): after = lax.ppermute(cells, AXES, [(i + 1, i) for i in range(ends)])  5.9 us
  transfers between devices with their start and end apart: 6, of which 0 were waited for; matrix products, arithmetic and copies ran while one was open for 2% of the time, Pallas kernels for 51%

profile of v1, /device:TPU:1, one launch (start us, length us, event | category | flops | bytes accessed | tf_op | source)
XLA Modules:
  0.0 213.8 jit_solution(1310154809828299302)
XLA Ops:
  0.0 1.0 pad_maximum_fusion.points_own
  1.0 0.0 copy-start.2
  1.0 4.6 %collective-permute-start.2 = (f32[4,48,256]{2,1,0:T(8,128)S(1)}, f32[4,48,256]{2,1,0:T(8,128)S(1)}, u32[]{:S(2)}, u32[]{:S(2)}) collective-permute-start(f32[4,48,256]{2,1,0:T(8,128)S(1)} %pad_maximum_fusion.points_own), channel_id=1, source_target_pairs={{0,1},{1,2},{2,3},{3,4},{4,5},{5,6},{6,7},{7,8},{8,9},{9,10},{10,1... | collective-permute-start | bytes 589832 | tf_op jit(solution)/shard_map/ppermute | solution.py:23
  5.6 1.9 collective-permute-start.3
  7.5 3.6 %collective-permute-start.4 = (f32[48,8,256]{2,1,0:T(8,128)}, f32[48,8,256]{2,1,0:T(8,128)S(1)}, u32[]{:S(2)}, u32[]{:S(2)}) collective-permute-start(f32[48,8,256]{2,1,0:T(8,128)} %vectors_own.1), channel_id=1, source_target_pairs={{0,1},{1,2},{2,3},{3,4},{4,5},{5,6},{6,7},{7,8},{8,9},{9,10},{10,1... | collective-permute-start | bytes 1179656 | tf_op jit(solution)/shard_map/ppermute | solution.py:23
  11.1 1.9 collective-permute-start.5
  13.1 6.9 %upward.1 = (f32[48,8,64]{2,1,0:T(8,128)}, f32[6,8,64]{2,1,0:T(8,128)}) custom-call(f32[48,8,256]{2,1,0:T(8,128)} %vectors_own.1, f32[48,64,256]{2,1,0:T(8,128)} %bitcast.3, f32[48,64,64]{2,1,0:T(8,128)} %transfer.3), custom_call_target="tpu_custom_call" | custom-call | flops 100663296 | bytes 9437184 | tf_op jit(solution)/shard_map/upward/pallas_call | solution.py:271
  20.0 3.6 %collective-permute-start = (f32[48,8,64]{2,1,0:T(8,128)}, f32[48,8,64]{2,1,0:T(8,128)S(1)}, u32[]{:S(2)}, u32[]{:S(2)}) collective-permute-start(f32[48,8,64]{2,1,0:T(8,128)} %get-tuple-element.7.coefs_own), channel_id=1, source_target_pairs={{0,1},{1,2},{2,3},{3,4},{4,5},{5,6},{6,7},{7,8},{8,9},{9,10},{10,1... | collective-permute-start | bytes 294920 | tf_op jit(solution)/shard_map/ppermute | solution.py:23
  23.6 0.8 copy.15
  24.4 0.8 copy.17
  25.2 0.6 subtract_select_fusion
  25.8 1.3 compare_select_fusion.coarse_slots
  27.1 46.6 %all_gather.3.every = f32[192,8,64]{2,1,0:T(8,128)} all-gather(f32[6,8,64]{2,1,0:T(8,128)} %get-tuple-element.8), channel_id=1, replica_groups=mesh['leaf'=4,'sub'=8] {'leaf','sub'}, dimensions={0}, use_global_device_ids=true | all-gather | bytes 405504 | tf_op jit(solution)/shard_map/all_gather | solution.py:292
  73.7 0.0 collective-permute-done.2.points_before
  73.7 0.0 copy-start.5
  73.7 2.1 collective-permute-start.1
  75.7 0.0 collective-permute-done.3.points_after
  75.8 0.0 copy-start.6
  75.8 0.0 collective-permute-done.4.vectors_before
  75.8 0.0 copy-start.3
  75.8 0.0 collective-permute-done.5.vectors_after
  75.8 0.0 copy-start.4
  75.8 0.0 copy-done.2
  75.8 0.0 copy-done.5
  75.8 0.6 copy-done.6
  76.4 0.1 copy-done.3
  76.6 0.1 copy-done.4
  76.7 102.1 %near_field.1.near = f32[48,8,256]{2,1,0:T(8,128)} custom-call(s32[48,16]{1,0:T(8,128)} %get-tuple-element.9.slots, f32[4,48,256]{2,1,0:T(8,128)} %copy-done.5, f32[4,48,256]{2,1,0:T(8,128)} %copy-done.2, f32[4,48,256]{2,1,0:T(8,128)} %copy-done.6, f32[48,8,256]{2,1,0:T(8,128)} %copy-done.3, f32[48,8,256]{2,1,0:T(8,128)} %vectors_own.1, f32[48,8,256]{2,1,0:T(8,128)} %copy-done.4), custom_call_target="tpu_custom_call" | custom-call | flops 25769803776 | bytes 1966080 | tf_op jit(solution)/shard_map/near_field/pallas_call | solution.py:300
  178.8 0.0 collective-permute-done.coefs_before
  178.8 0.0 copy-start
  178.8 0.0 collective-permute-done.1.coefs_after
  178.8 0.0 copy-start.1
  178.8 0.7 copy-done
  179.5 0.1 copy-done.1
  179.6 34.2 %far_field.1 = f32[48,8,256]{2,1,0:T(8,128)} custom-call(s32[48,16]{1,0:T(8,128)} %get-tuple-element.10.far_slots, s32[6,32]{1,0:T(8,128)} %compare_select_fusion.coarse_slots, f32[48,8,64]{2,1,0:T(8,128)} %copy-done, f32[48,8,64]{2,1,0:T(8,128)} %get-tuple-element.7.coefs_own, f32[48,8,64]{2,1,0:T(8,128)} %copy-done.1, f32[192,8,64]{2,1,0:T(8,128)} %all_gather.3.every, ...), custom_call_target="tpu_custom_call" | custom-call | flops 201326592 | bytes 25165824 | tf_op jit(solution)/shard_map/far_field/pallas_call | solution.py:328
Async XLA Ops:
  1.0 74.9 %copy-start.2 = (f32[4,48,256]{2,1,0:T(8,128)}, f32[4,48,256]{2,1,0:T(8,128)S(1)}, u32[]{:S(2)}) copy-start(f32[4,48,256]{2,1,0:T(8,128)S(1)} %pad_maximum_fusion.points_own) | copy-start | bytes 589828
  1.0 72.7 %collective-permute-start.2 = (f32[4,48,256]{2,1,0:T(8,128)S(1)}, f32[4,48,256]{2,1,0:T(8,128)S(1)}, u32[]{:S(2)}, u32[]{:S(2)}) collective-permute-start(f32[4,48,256]{2,1,0:T(8,128)S(1)} %pad_maximum_fusion.points_own), channel_id=1, source_target_pairs={{0,1},{1,2},{2,3},{3,4},{4,5},{5,6},{6,7},{7,8},{8,9},{9,10},{10,1... | collective-permute-start | bytes 589832 | tf_op jit(solution)/shard_map/ppermute | solution.py:23
  5.6 70.2 %collective-permute-start.3 = (f32[4,48,256]{2,1,0:T(8,128)S(1)}, f32[4,48,256]{2,1,0:T(8,128)S(1)}, u32[]{:S(2)}, u32[]{:S(2)}) collective-permute-start(f32[4,48,256]{2,1,0:T(8,128)S(1)} %pad_maximum_fusion.points_own), channel_id=1, source_target_pairs={{1,0},{2,1},{3,2},{4,3},{5,4},{6,5},{7,6},{8,7},{9,8},{10,9},{11,1... | collective-permute-start | bytes 589832 | tf_op jit(solution)/shard_map/ppermute | solution.py:24
  7.5 68.3 %collective-permute-start.4 = (f32[48,8,256]{2,1,0:T(8,128)}, f32[48,8,256]{2,1,0:T(8,128)S(1)}, u32[]{:S(2)}, u32[]{:S(2)}) collective-permute-start(f32[48,8,256]{2,1,0:T(8,128)} %vectors_own.1), channel_id=1, source_target_pairs={{0,1},{1,2},{2,3},{3,4},{4,5},{5,6},{6,7},{7,8},{8,9},{9,10},{10,1... | collective-permute-start | bytes 1179656 | tf_op jit(solution)/shard_map/ppermute | solution.py:23
  11.1 64.6 %collective-permute-start.5 = (f32[48,8,256]{2,1,0:T(8,128)}, f32[48,8,256]{2,1,0:T(8,128)S(1)}, u32[]{:S(2)}, u32[]{:S(2)}) collective-permute-start(f32[48,8,256]{2,1,0:T(8,128)} %vectors_own.1), channel_id=1, source_target_pairs={{1,0},{2,1},{3,2},{4,3},{5,4},{6,5},{7,6},{8,7},{9,8},{10,9},{11,1... | collective-permute-start | bytes 1179656 | tf_op jit(solution)/shard_map/ppermute | solution.py:24
  20.0 158.8 %collective-permute-start = (f32[48,8,64]{2,1,0:T(8,128)}, f32[48,8,64]{2,1,0:T(8,128)S(1)}, u32[]{:S(2)}, u32[]{:S(2)}) collective-permute-start(f32[48,8,64]{2,1,0:T(8,128)} %get-tuple-element.7.coefs_own), channel_id=1, source_target_pairs={{0,1},{1,2},{2,3},{3,4},{4,5},{5,6},{6,7},{7,8},{8,9},{9,10},{10,1... | collective-permute-start | bytes 294920 | tf_op jit(solution)/shard_map/ppermute | solution.py:23
  73.7 2.1 %copy-start.5 = (f32[4,48,256]{2,1,0:T(8,128)}, f32[4,48,256]{2,1,0:T(8,128)S(1)}, u32[]{:S(2)}) copy-start(f32[4,48,256]{2,1,0:T(8,128)S(1)} %collective-permute-done.2.points_before) | copy-start | bytes 589828
  73.7 105.1 %collective-permute-start.1 = (f32[48,8,64]{2,1,0:T(8,128)}, f32[48,8,64]{2,1,0:T(8,128)S(1)}, u32[]{:S(2)}, u32[]{:S(2)}) collective-permute-start(f32[48,8,64]{2,1,0:T(8,128)} %get-tuple-element.7.coefs_own), channel_id=1, source_target_pairs={{1,0},{2,1},{3,2},{4,3},{5,4},{6,5},{7,6},{8,7},{9,8},{10,9},{11,1... | collective-permute-start | bytes 294920 | tf_op jit(solution)/shard_map/ppermute | solution.py:24
  75.8 0.7 copy-start.6
  75.8 0.8 copy-start.3
  75.8 0.9 copy-start.4
  178.8 0.7 copy-start
  178.8 0.8 copy-start.1

commit v2 on v1

--- a/solution.py
+++ b/solution.py
@@ -1,3 +1,4 @@
+import functools
 import math
 
 import jax
@@ -18,13 +19,6 @@
 bf16 = jnp.bfloat16
 
 
-def halo(cells):
-    ends = lax.axis_size(AXES) - 1
-    before = lax.ppermute(cells, AXES, [(i, i + 1) for i in range(ends)])
-    after = lax.ppermute(cells, AXES, [(i + 1, i) for i in range(ends)])
-    return before, after
-
-
 def three(x):
     high = x.astype(bf16).astype(f32)
     rest = x - high
@@ -55,17 +49,120 @@
     return x[:half] + x[half:]
 
 
-def up_kernel(vectors, basis, transfer, coefs, parents):
-    total = jnp.zeros((16, transfer.shape[2]), f32)
-    for q in range(CHILDREN):
-        high, low = split(basis[q])
-        rows = stacked_rows(vectors[q])
-        one = folded(dot_t(rows, high) + dot_t(rows, low))
-        coefs[q] = one
-        rows = stacked_rows(one)
-        high, low = split(transfer[q])
-        total = total + dot(rows, high) + dot(rows, low)
-    parents[0] = folded(total)
+def packed(parent):
+    half = parent.shape[0] // 2
+    return jnp.concatenate([parent[:half], parent[half:]], axis=1)
+
+
+def unpacked(half):
+    rank = half.shape[1] // 2
+    return jnp.concatenate([half[:, :rank], half[:, rank:]], axis=0)
+
+
+def exchange_kernel(
+    count,
+    sites,
+    vectors,
+    basis,
+    transfer,
+    sites_before,
+    sites_after,
+    vectors_before,
+    vectors_after,
+    coefs,
+    coefs_before,
+    coefs_after,
+    every,
+    halo_send,
+    halo_recv,
+    all_send,
+    all_recv,
+):
+    inner = lax.axis_size("sub")
+    me = lax.axis_index("leaf") * inner + lax.axis_index("sub")
+    pairs = every.shape[0] // count
+    mine = every.at[pl.ds(me * pairs, pairs)]
+
+    def device(step):
+        to = lax.rem(me + step, count)
+        return (to // inner, lax.rem(to, inner))
+
+    barrier = pltpu.get_barrier_semaphore()
+
+    def greet(step, carry):
+        pl.semaphore_signal(
+            barrier, inc=1, device_id=device(step), device_id_type=pl.DeviceIdType.MESH
+        )
+        return carry
+
+    lax.fori_loop(1, count, greet, 0)
+    pl.semaphore_wait(barrier, count - 1)
+
+    def send(at, source, target, step):
+        return pltpu.make_async_remote_copy(
+            src_ref=source,
+            dst_ref=target,
+            send_sem=halo_send.at[at],
+            recv_sem=halo_recv.at[at],
+            device_id=device(step),
+            device_id_type=pl.DeviceIdType.MESH,
+        )
+
+    right, left = 1, count - 1
+    copies = [
+        send(0, sites, sites_before, right),
+        send(1, sites, sites_after, left),
+        send(2, vectors, vectors_before, right),
+        send(3, vectors, vectors_after, left),
+    ]
+    for copy in copies:
+        copy.start()
+
+    def upward(parent):
+        total = jnp.zeros((16, transfer.shape[2]), f32)
+        for q in range(CHILDREN):
+            at = parent * CHILDREN + q
+            high, low = split(basis[at])
+            rows = stacked_rows(vectors[at])
+            one = folded(dot_t(rows, high) + dot_t(rows, low))
+            coefs[at] = one
+            rows = stacked_rows(one)
+            high, low = split(transfer[at])
+            total = total + dot(rows, high) + dot(rows, low)
+        return packed(folded(total))
+
+    def pair(at, carry):
+        every[me * pairs + at] = jnp.concatenate([upward(2 * at), upward(2 * at + 1)], axis=0)
+        return carry
+
+    lax.fori_loop(0, pairs, pair, 0)
+
+    late = [send(4, coefs, coefs_before, right), send(5, coefs, coefs_after, left)]
+    for copy in late:
+        copy.start()
+
+    def share(step):
+        return pltpu.make_async_remote_copy(
+            src_ref=mine,
+            dst_ref=mine,
+            send_sem=all_send.at[step - 1],
+            recv_sem=all_recv.at[step - 1],
+            device_id=device(step),
+            device_id_type=pl.DeviceIdType.MESH,
+        )
+
+    def begin(step, carry):
+        share(step).start()
+        return carry
+
+    def finish(step, carry):
+        share(step).wait()
+        return carry
+
+    lax.fori_loop(1, count, begin, 0)
+    for copy in copies + late:
+        copy.wait()
+    lax.fori_loop(1, count, finish, 0)
 
 
 def pieces(points, at):
@@ -148,10 +245,14 @@
             return total
 
         total = jnp.zeros((16, out.shape[2]), f32)
-        fours = (count + 1) // 4
-        total = lax.fori_loop(0, fours, lambda g, t: some(4 * g, 4, t), total)
-        twos = jnp.where(count > 4 * fours, 1, 0)
-        total = lax.fori_loop(0, twos, lambda g, t: some(4 * fours, 2, t), total)
+        eights = count // 8
+        total = lax.fori_loop(0, eights, lambda g, t: some(8 * g, 8, t), total)
+        pairs = (count - 8 * eights + 1) // 2
+        for many in range(1, 5):
+            trips = jnp.where(pairs == many, 1, 0)
+            total = lax.fori_loop(
+                0, trips, lambda g, t, many=many: some(8 * eights, 2 * many, t), total
+            )
         out[q] = folded(total) * (gain * points_own[3, pl.ds(base + q, 1), :])
         return carry
 
@@ -198,13 +299,16 @@
             return carry
 
         def prepare_parent(at, carry):
-            parents[at] = stacked_rows(every[at])
+            both = every[at]
+            half = both.shape[0] // 2
+            parents[2 * at] = stacked_rows(unpacked(both[:half]))
+            parents[2 * at + 1] = stacked_rows(unpacked(both[half:]))
             return carry
 
         lax.fori_loop(0, ldev, prepare, 0, unroll=2)
         lax.fori_loop(0, every.shape[0], prepare_parent, 0, unroll=4)
         coefs[3 * ldev] = jnp.zeros(coefs.shape[1:], bf16)
-        parents[every.shape[0]] = jnp.zeros(parents.shape[1:], bf16)
+        parents[2 * every.shape[0]] = jnp.zeros(parents.shape[1:], bf16)
 
     field = coupled(
         step, coarse_slots, parents, lambda k: coarse[0, k : k + 4].reshape(4 * rank, rank)
@@ -265,36 +369,51 @@
 
     basis = basis.swapaxes(1, 2)
     sites = jnp.concatenate([points.swapaxes(0, 1), amplitude[None]], axis=0)
-    points_before, points_after = halo(sites)
-    vectors_before, vectors_after = halo(vectors)
-
-    coefs, parents = pl.pallas_call(
-        up_kernel,
-        grid=(nparents,),
-        out_shape=(
-            jax.ShapeDtypeStruct((ldev, count, rank), f32),
-            jax.ShapeDtypeStruct((nparents, count, rank), f32),
+    devices = lax.axis_size(AXES)
+    results = (
+        sites.shape,
+        sites.shape,
+        vectors.shape,
+        vectors.shape,
+        (ldev, count, rank),
+        (ldev, count, rank),
+        (ldev, count, rank),
+        (devices * nparents // 2, count, 2 * rank),
+    )
+    (
+        points_before,
+        points_after,
+        vectors_before,
+        vectors_after,
+        coefs,
+        coefs_before,
+        coefs_after,
+        every,
+    ) = pl.pallas_call(
+        functools.partial(exchange_kernel, devices),
+        out_shape=tuple(jax.ShapeDtypeStruct(shape, f32) for shape in results),
+        in_specs=[pl.BlockSpec(memory_space=pltpu.VMEM)] * 4,
+        out_specs=tuple(pl.BlockSpec(memory_space=pltpu.VMEM) for _ in results),
+        scratch_shapes=[
+            pltpu.SemaphoreType.DMA((6,)),
+            pltpu.SemaphoreType.DMA((6,)),
+            pltpu.SemaphoreType.DMA((devices - 1,)),
+            pltpu.SemaphoreType.DMA((devices - 1,)),
+        ],
+        compiler_params=pltpu.CompilerParams(
+            vmem_limit_bytes=VMEM_BYTES, collective_id=0, has_side_effects=True
         ),
-        in_specs=[part(vectors, CHILDREN), part(basis, CHILDREN), part(transfer, CHILDREN)],
-        out_specs=(
-            pl.BlockSpec((CHILDREN, count, rank), lambda i: (i, 0, 0)),
-            pl.BlockSpec((1, count, rank), lambda i: (i, 0, 0)),
-        ),
-        compiler_params=params(),
         cost_estimate=pl.CostEstimate(
             flops=8 * ldev * leaf_size * rank * 16,
             bytes_accessed=12 * ldev * leaf_size * rank,
             transcendentals=0,
         ),
-        name="upward",
-    )(vectors, basis, transfer)
-
-    every = lax.all_gather(parents, AXES, axis=0, tiled=True)
-    coefs_before, coefs_after = halo(coefs)
+        name="upward_exchange",
+    )(sites, vectors, basis, transfer)
 
     near_slots = jnp.where(near_list >= 0, near_list - offset, blank)
     far_slots = jnp.where(far_list >= 0, far_list - offset, blank)
-    coarse_slots = jnp.where(coarse_list >= 0, coarse_list, every.shape[0])
+    coarse_slots = jnp.where(coarse_list >= 0, coarse_list, 2 * every.shape[0])
 
     pairs = ldev * near_list.shape[1]
     near = pl.pallas_call(
@@ -345,7 +464,7 @@
         out_specs=pl.BlockSpec((CHILDREN, count, leaf_size), lambda i: (i, 0, 0)),
         scratch_shapes=[
             pltpu.VMEM((blank + 1, 2 * count, rank), bf16),
-            pltpu.VMEM((every.shape[0] + 1, 2 * count, rank), bf16),
+            pltpu.VMEM((2 * every.shape[0] + 1, 2 * count, rank), bf16),
         ],
         compiler_params=params(),
         cost_estimate=pl.CostEstimate(

time: 217 us -> 159 us (0.73)
  blocking collectives: 46.6 us -> 0 us
  starting transfers between devices: 17.8 us -> 0 us
  Pallas kernels: 143 us -> 153 us
    all_gather x1 -> x0, blocking collectives: 46.6 us -> none  [on_device(): every = lax.all_gather(parents, AXES, axis=0, tiled=True)]
    pallas_call x1, Pallas kernels: 6.92 us -> 37.6 us  [on_device(): pl.pallas_call(functools.partial(exchange_kernel, devices), out_shape=tup...]
    pallas_call x1, Pallas kernels: 102 us -> 80 us  [on_device(): pl.pallas_call(near_kernel, grid=(nparents,), out_shape=jax.ShapeDtypeStr...]
    ppermute x6 -> x0, starting transfers between devices: 17.8 us -> none  [the longest x3 11.9 us: halo(): before = lax.ppermute(cells, AXES, [(i, i + 1) for i in range(ends)])]
  transfers between devices with their start and end apart: 6 -> 0, of which waited for: 0 -> 0; matrix products, arithmetic and copies ran while one was open for 2% -> 0% of each run, Pallas kernels for 51% -> 0%
where the time goes in v2:
time: 159 us; the launch traced here: 158 us
  Pallas kernels  153 us (96%)
  other arithmetic  2.83 us (2%)
    pallas_call x1, Pallas kernels, on_device(): pl.pallas_call(near_kernel, grid=(nparents,), out_shape=jax.ShapeDtypeStr...  80 us
    pallas_call x1, Pallas kernels, on_device(): pl.pallas_call(functools.partial(exchange_kernel, devices), out_shape=tup...  37.6 us
    pallas_call x1, Pallas kernels, on_device(): pl.pallas_call(far_kernel, grid=(nparents,), out_shape=jax.ShapeDtypeStru...  35.7 us

profile of v2, /device:TPU:1, one launch (start us, length us, event | category | flops | bytes accessed | tf_op | source)
XLA Modules:
  0.0 157.7 jit_solution(8650588436534180583)
XLA Ops:
  0.0 1.6 %pad_maximum_fusion.sites.points_own = f32[4,48,256]{2,1,0:T(8,128)} fusion(f32[1,48,256]{2,1,0:T(8,128)} %bitcast.6, f32[3,48,256]{2,1,0:T(8,128)} %bitcast.5), kind=kLoop, calls=%fused_computation | loop fusion | flops 49152 | bytes 393216 | tf_op jit(solution)/shard_map/concatenate | solution.py:371
  1.6 37.6 %upward_exchange.1 = (f32[4,48,256]{2,1,0:T(8,128)}, f32[4,48,256]{2,1,0:T(8,128)}, f32[48,8,256]{2,1,0:T(8,128)}, f32[48,8,256]{2,1,0:T(8,128)}, f32[48,8,64]{2...) custom-call(f32[4,48,256]{2,1,0:T(8,128)} %pad_maximum_fusion.sites.points_own, ...), custom_call_target="tpu_custom_call" | custom-call | flops 100663296 | bytes 9437184 | tf_op jit(solution)/shard_map/upward_exchange/pallas_call | solution.py:392
  39.3 0.8 copy.11
  40.0 0.8 copy.13
  40.8 0.6 subtract_select_fusion
  41.4 0.0 copy-start
  41.4 80.0 %near_field.1.near = f32[48,8,256]{2,1,0:T(8,128)} custom-call(s32[48,16]{1,0:T(8,128)} %get-tuple-element.21.slots, f32[4,48,256]{2,1,0:T(8,128)} %get-tuple-element.17.points_before, f32[4,48,256]{2,1,0:T(8,128)} %pad_maximum_fusion.sites.points_own, f32[4,48,256]{2,1,0:T(8,128)} %get-tuple-element.18.points_after, ...), custom_call_target="tpu_custom_call" | custom-call | flops 25769803776 | bytes 1966080 | tf_op jit(solution)/shard_map/near_field/pallas_call | solution.py:419
  121.5 0.0 copy-done
  121.5 0.6 compare_select_fusion.coarse_slots
  122.0 35.7 %far_field.1 = f32[48,8,256]{2,1,0:T(8,128)} custom-call(s32[48,16]{1,0:T(8,128)} %get-tuple-element.22.far_slots, s32[6,32]{1,0:T(8,128)} %compare_select_fusion.coarse_slots, f32[48,8,64]{2,1,0:T(8,128)} %get-tuple-element.13.coefs_before, f32[48,8,64]{2,1,0:T(8,128)} %get-tuple-element.14.coefs_own, f32[48,8,64]{2,1,0:T(8,128)} %get-tuple-element.15.coefs_after, ...), custom_call_target="tpu_custom_call" | custom-call | flops 201326592 | bytes 25165824 | tf_op jit(solution)/shard_map/far_field/pallas_call | solution.py:447
Async XLA Ops:
  41.4 80.0 %copy-start = (s32[6,32]{1,0:T(8,128)S(1)}, s32[6,32]{1,0:T(8,128)}, u32[]{:S(2)}) copy-start(s32[6,32]{1,0:T(8,128)} %param.19) | copy-start | bytes 2308

commit v3 on v2

--- a/solution.py
+++ b/solution.py
@@ -12,6 +12,8 @@
 NEAR = 16
 ELL2 = 0.25
 AXES = ("leaf", "sub")
+FAR_UNROLL = 2
+PREPARE_UNROLL = 2
 CHILDREN = 8
 FEATURES = 32
 VMEM_BYTES = 56 * 1024 * 1024
@@ -218,7 +220,7 @@
                 values[where] = stacked_rows(vectors[at] * points[3, pl.ds(at, 1), :])
             return carry
 
-        lax.fori_loop(0, ldev, prepare, 0)
+        lax.fori_loop(0, ldev, prepare, 0, unroll=PREPARE_UNROLL)
         others[blank] = jnp.zeros(others.shape[1:], bf16)
         values[blank] = jnp.zeros(values.shape[1:], bf16)
 
@@ -262,10 +264,16 @@
 def coupled(index, slots, table, matrix):
     rank = table.shape[2]
     total = jnp.zeros((64, 4 * rank), f32)
-    for g in range(slots.shape[1] // 4):
-        rows = jnp.concatenate([table[slots[index, 4 * g + u]] for u in range(4)], axis=0)
-        high, low = split(matrix(4 * g))
-        total = total + dot_t(rows, high) + dot_t(rows, low)
+    for g in range(0, slots.shape[1], 8):
+        left, right = [], []
+        for first in (g, g + 4):
+            rows = jnp.concatenate([table[slots[index, first + u]] for u in range(4)], axis=0)
+            left += [rows, rows]
+            full = matrix(first)
+            high = full.astype(bf16).astype(f32)
+            right += [high, full - high]
+        right = jnp.concatenate(right, axis=1).astype(bf16)
+        total = total + dot_t(jnp.concatenate(left, axis=1), right)
     blocks = [total[16 * u : 16 * u + 16, rank * u : rank * u + rank] for u in range(4)]
     return folded(blocks[0] + blocks[1] + blocks[2] + blocks[3])
 
@@ -329,7 +337,7 @@
         out[q] = near[q] + folded(dot(rows, high) + dot(rows, low))
         return carry
 
-    lax.fori_loop(0, CHILDREN, leaf, 0)
+    lax.fori_loop(0, CHILDREN, leaf, 0, unroll=FAR_UNROLL)
 
 
 def whole(x):

time: 159 us -> 151 us (0.950)
  Pallas kernels: 153 us -> 144 us
    pallas_call x1, Pallas kernels: 35.7 us -> 30.6 us  [on_device(): pl.pallas_call(far_kernel, grid=(nparents,), out_shape=jax.ShapeDtypeStru...]
    pallas_call x1, Pallas kernels: 80 us -> 75.6 us  [on_device(): pl.pallas_call(near_kernel, grid=(nparents,), out_shape=jax.ShapeDtypeStr...]
where the time goes in v3:
time: 151 us; the launch traced here: 148 us
  Pallas kernels  144 us (95%)
  other arithmetic  2.83 us (2%)
  local copies, waits for them, and re-layouts  1.56 us (1%)
    pallas_call x1, Pallas kernels, on_device(): pl.pallas_call(near_kernel, grid=(nparents,), out_shape=jax.ShapeDtypeStr...  75.6 us
    pallas_call x1, Pallas kernels, on_device(): pl.pallas_call(functools.partial(exchange_kernel, devices), out_shape=tup...  37.6 us
    pallas_call x1, Pallas kernels, on_device(): pl.pallas_call(far_kernel, grid=(nparents,), out_shape=jax.ShapeDtypeStru...  30.6 us

profile of v3, /device:TPU:1, one launch (start us, length us, event | category | flops | bytes accessed | tf_op | source)
XLA Modules:
  0.0 148.3 jit_solution(4216515415810430000)
XLA Ops:
  0.0 1.6 %pad_maximum_fusion.sites.points_own = f32[4,48,256]{2,1,0:T(8,128)} fusion(f32[1,48,256]{2,1,0:T(8,128)} %bitcast.6, f32[3,48,256]{2,1,0:T(8,128)} %bitcast.5), kind=kLoop, calls=%fused_computation | loop fusion | flops 49152 | bytes 393216 | tf_op jit(solution)/shard_map/concatenate | solution.py:379
  1.6 37.6 %upward_exchange.1 = (f32[4,48,256]{2,1,0:T(8,128)}, f32[4,48,256]{2,1,0:T(8,128)}, f32[48,8,256]{2,1,0:T(8,128)}, f32[48,8,256]{2,1,0:T(8,128)}, f32[48,8,64]{2...) custom-call(f32[4,48,256]{2,1,0:T(8,128)} %pad_maximum_fusion.sites.points_own, ...), custom_call_target="tpu_custom_call" | custom-call | flops 100663296 | bytes 9437184 | tf_op jit(solution)/shard_map/upward_exchange/pallas_call | solution.py:400
  39.3 0.8 copy.11
  40.0 0.8 copy.13
  40.8 0.6 subtract_select_fusion
  41.4 0.0 copy-start
  41.4 75.6 %near_field.1.near = f32[48,8,256]{2,1,0:T(8,128)} custom-call(s32[48,16]{1,0:T(8,128)} %get-tuple-element.21.slots, f32[4,48,256]{2,1,0:T(8,128)} %get-tuple-element.17.points_before, f32[4,48,256]{2,1,0:T(8,128)} %pad_maximum_fusion.sites.points_own, f32[4,48,256]{2,1,0:T(8,128)} %get-tuple-element.18.points_after, ...), custom_call_target="tpu_custom_call" | custom-call | flops 25769803776 | bytes 1966080 | tf_op jit(solution)/shard_map/near_field/pallas_call | solution.py:427
  117.1 0.0 copy-done
  117.1 0.6 compare_select_fusion.coarse_slots
  117.7 30.6 %far_field.1 = f32[48,8,256]{2,1,0:T(8,128)} custom-call(s32[48,16]{1,0:T(8,128)} %get-tuple-element.22.far_slots, s32[6,32]{1,0:T(8,128)} %compare_select_fusion.coarse_slots, f32[48,8,64]{2,1,0:T(8,128)} %get-tuple-element.13.coefs_before, f32[48,8,64]{2,1,0:T(8,128)} %get-tuple-element.14.coefs_own, f32[48,8,64]{2,1,0:T(8,128)} %get-tuple-element.15.coefs_after, ...), custom_call_target="tpu_custom_call" | custom-call | flops 201326592 | bytes 25165824 | tf_op jit(solution)/shard_map/far_field/pallas_call | solution.py:455
Async XLA Ops:
  41.4 75.6 %copy-start = (s32[6,32]{1,0:T(8,128)S(1)}, s32[6,32]{1,0:T(8,128)}, u32[]{:S(2)}) copy-start(s32[6,32]{1,0:T(8,128)} %param.19) | copy-start | bytes 2308

commit v4 on v3

--- a/solution.py
+++ b/solution.py
@@ -117,8 +117,40 @@
         send(2, vectors, vectors_before, right),
         send(3, vectors, vectors_after, left),
     ]
-    for copy in copies:
-        copy.start()
+    has_right, has_left = me < count - 1, me > 0
+
+    def start(pair):
+        @pl.when(has_right)
+        def _():
+            pair[0].start()
+
+        @pl.when(has_left)
+        def _():
+            pair[1].start()
+
+    def wait(pair):
+        @pl.when(has_right)
+        def _():
+            pair[0].wait_send()
+            pair[1].wait_recv()
+
+        @pl.when(has_left)
+        def _():
+            pair[1].wait_send()
+            pair[0].wait_recv()
+
+    start(copies[:2])
+    start(copies[2:])
+
+    @pl.when(me == 0)
+    def _():
+        for ref in (sites_before, vectors_before, coefs_before):
+            ref[...] = jnp.zeros(ref.shape, f32)
+
+    @pl.when(me == count - 1)
+    def _():
+        for ref in (sites_after, vectors_after, coefs_after):
+            ref[...] = jnp.zeros(ref.shape, f32)
 
     def upward(parent):
         total = jnp.zeros((16, transfer.shape[2]), f32)
@@ -140,8 +172,7 @@
     lax.fori_loop(0, pairs, pair, 0)
 
     late = [send(4, coefs, coefs_before, right), send(5, coefs, coefs_after, left)]
-    for copy in late:
-        copy.start()
+    start(late)
 
     def share(step):
         return pltpu.make_async_remote_copy(
@@ -162,8 +193,9 @@
         return carry
 
     lax.fori_loop(1, count, begin, 0)
-    for copy in copies + late:
-        copy.wait()
+    wait(copies[:2])
+    wait(copies[2:])
+    wait(late)
     lax.fori_loop(1, count, finish, 0)
 
 

time: 151 us -> 152 us (level); the launches traced: 148 us -> 151 us
  Pallas kernels: 144 us -> 147 us
    pallas_call x1, Pallas kernels: 75.6 us -> 78.4 us  [on_device(): pl.pallas_call(near_kernel, grid=(nparents,), out_shape=jax.ShapeDtypeStr...]
where the time goes in v4:
time: 152 us; the launch traced here: 151 us
  Pallas kernels  147 us (97%)
  other arithmetic  2.83 us (2%)
  local copies, waits for them, and re-layouts  1.56 us (1%)
    pallas_call x1, Pallas kernels, on_device(): pl.pallas_call(near_kernel, grid=(nparents,), out_shape=jax.ShapeDtypeStr...  78.4 us
    pallas_call x1, Pallas kernels, on_device(): pl.pallas_call(functools.partial(exchange_kernel, devices), out_shape=tup...  37.6 us
    pallas_call x1, Pallas kernels, on_device(): pl.pallas_call(far_kernel, grid=(nparents,), out_shape=jax.ShapeDtypeStru...  30.6 us

profile of v4, /device:TPU:1, one launch (start us, length us, event | category | flops | bytes accessed | tf_op | source)
XLA Modules:
  0.0 151.0 jit_solution(9617977963921675017)
XLA Ops:
  0.0 1.6 %pad_maximum_fusion.sites.points_own = f32[4,48,256]{2,1,0:T(8,128)} fusion(f32[1,48,256]{2,1,0:T(8,128)} %bitcast.6, f32[3,48,256]{2,1,0:T(8,128)} %bitcast.5), kind=kLoop, calls=%fused_computation | loop fusion | flops 49152 | bytes 393216 | tf_op jit(solution)/shard_map/concatenate | solution.py:411
  1.6 37.6 %upward_exchange.1 = (f32[4,48,256]{2,1,0:T(8,128)}, f32[4,48,256]{2,1,0:T(8,128)}, f32[48,8,256]{2,1,0:T(8,128)}, f32[48,8,256]{2,1,0:T(8,128)}, f32[48,8,64]{2...) custom-call(f32[4,48,256]{2,1,0:T(8,128)} %pad_maximum_fusion.sites.points_own, ...), custom_call_target="tpu_custom_call" | custom-call | flops 100663296 | bytes 9437184 | tf_op jit(solution)/shard_map/upward_exchange/pallas_call | solution.py:432
  39.3 0.8 copy.11
  40.0 0.8 copy.13
  40.8 0.6 subtract_select_fusion
  41.4 0.0 copy-start
  41.4 78.4 %near_field.1.near = f32[48,8,256]{2,1,0:T(8,128)} custom-call(s32[48,16]{1,0:T(8,128)} %get-tuple-element.21.slots, f32[4,48,256]{2,1,0:T(8,128)} %get-tuple-element.17.points_before, f32[4,48,256]{2,1,0:T(8,128)} %pad_maximum_fusion.sites.points_own, f32[4,48,256]{2,1,0:T(8,128)} %get-tuple-element.18.points_after, ...), custom_call_target="tpu_custom_call" | custom-call | flops 25769803776 | bytes 1966080 | tf_op jit(solution)/shard_map/near_field/pallas_call | solution.py:459
  119.8 0.0 copy-done
  119.8 0.6 compare_select_fusion.coarse_slots
  120.4 30.6 %far_field.1 = f32[48,8,256]{2,1,0:T(8,128)} custom-call(s32[48,16]{1,0:T(8,128)} %get-tuple-element.22.far_slots, s32[6,32]{1,0:T(8,128)} %compare_select_fusion.coarse_slots, f32[48,8,64]{2,1,0:T(8,128)} %get-tuple-element.13.coefs_before, f32[48,8,64]{2,1,0:T(8,128)} %get-tuple-element.14.coefs_own, f32[48,8,64]{2,1,0:T(8,128)} %get-tuple-element.15.coefs_after, ...), custom_call_target="tpu_custom_call" | custom-call | flops 201326592 | bytes 25165824 | tf_op jit(solution)/shard_map/far_field/pallas_call | solution.py:487
Async XLA Ops:
  41.4 78.4 %copy-start = (s32[6,32]{1,0:T(8,128)S(1)}, s32[6,32]{1,0:T(8,128)}, u32[]{:S(2)}) copy-start(s32[6,32]{1,0:T(8,128)} %param.19) | copy-start | bytes 2308
